TPU v7x, 32 devices: a whole 2x2x4 slice. The times are simulated.
32 devices in a mesh: grp: 2 (over y), chan: 4 (over z), win: 2 (over x), rep: 2 (over core).
Axes of the slice: x: 2, y: 2, z: 4, core: 2. Of those that a mesh axis runs over, the one named last changes fastest.
Arguments:
- sources: bfloat16 [8, 256, 4096], P(('grp', 'chan'), None, 'win'), parts along dimension 0, may hold values from -6 to 6
- receivers: bfloat16 [32, 4096], P(('grp', 'chan'), 'win'), parts along dimension 0, may hold values from -6 to 6
- plan: int32 [2, 2], P('grp'), parts along dimension 0, may hold values from 0 to 3, as said below
- pair_index: int32 [2, 4, 4, 512], P('grp', 'chan'), parts along dimension 0, may hold values from 0 to 2047, as said below
- keep: int32 [2, 4, 4, 512], P('grp', 'chan'), parts along dimension 0, may hold values 0 or 1
Outputs:
- stacks: float32 [8, 1, 4, 512, 2048], P(('grp', 'chan'), None, None, None, ('win', 'rep')), parts along dimension 0
There are 2 independent parts, one for each index of `grp`. A program takes and returns all parts, laid end to end along the dimension named above; each array names one. Nothing has to cross between parts.
Inputs may be any that keep to these rules, and one draw needn't show every extreme that they name: `plan`: the entries of one round name different blocks. For each round k and group c, pair_index[k, c] names every number below 2048 exactly once.
All inputs are finite; a program needn't handle non-finite values. No bound on the sum of `keep` on one device may be relied on, other than what follows from the above.
Results may differ from a plain program's by a relative error of at most 0.0003.
Values may be sent and summed in bfloat16 or wider, within the bound.
No kernel may reach another device: no remote copies, remote signals or barrier semaphores. Data moves between devices by JAX's collectives and lax.ppermute only.
A program may use at most 64 MiB of HBM per device.

v0:
```python
import math

import jax
import jax.numpy as jnp
from jax import lax
from jax.sharding import PartitionSpec as P

LAGS = 2048


def broadcast(value, axis, source):
    kept = jnp.where(lax.axis_index(axis) == source, value, 0).astype(value.dtype)
    return lax.psum(kept, axis)


def from_behind(block, axis, distance):
    devices = range(lax.axis_size(axis))
    route = [(i - distance, i) for i in devices if i - distance in devices]
    return lax.ppermute(block, axis, route)


def fetch_block(sources, number, owned):
    own_block = lax.dynamic_index_in_dim(sources, number % owned, 0, keepdims=False)
    return broadcast(own_block, "chan", number // owned)


def lag_tile(window, lag_block, samples):
    rows, span = window.shape
    tiled = jnp.tile(window, (1, lag_block + 1))
    shifted = tiled[:, : lag_block * (span + 1)].reshape(rows, lag_block, span + 1)
    return shifted[:, :, :samples]


def correlate(source_rows, extended, rep_index, lag_dev, piece, lag_block, n_rep, samples):
    block_count = lag_dev // lag_block
    empty = jnp.zeros((source_rows.shape[0], extended.shape[0], lag_dev), jnp.float32)

    def lag_step(number, total):
        lag_start = number * lag_block
        first_lag = (lag_start // piece * n_rep + rep_index) * piece + lag_start % piece
        window = lax.dynamic_slice_in_dim(extended, first_lag, samples + lag_block, 1)
        toeplitz = lag_tile(window, lag_block, samples)
        partial_value = jnp.einsum(
            "st,rkt->srk", source_rows, toeplitz, preferred_element_type=jnp.float32
        )
        return lax.dynamic_update_slice_in_dim(total, partial_value, lag_start, 2)

    return lax.fori_loop(0, block_count, lag_step, empty)


def shards(sources, receivers, plan, pair_index, keep):
    owned, block_width, samples = sources.shape
    n_win = lax.axis_size("win")
    n_rep = lax.axis_size("rep")
    lag_dev = LAGS // n_rep
    piece = lag_dev // n_win
    lag_block = min(128, piece)
    rep_index = lax.axis_index("rep")
    tail_parts = [from_behind(receivers, "win", -1)]
    extended = jnp.concatenate([receivers] + tail_parts, axis=1)
    norming = 1.0 / math.sqrt(samples * n_win)
    block_one = fetch_block(sources, plan[0, 0], owned)
    block_two = fetch_block(sources, plan[0, 1], owned)
    source_rows = jnp.concatenate([block_one, block_two], axis=0)
    corr = correlate(source_rows, extended, rep_index, lag_dev, piece, lag_block, n_rep, samples)
    flattened = corr.reshape(-1, lag_dev) * norming
    selected = jnp.take(flattened, pair_index[0, 0], axis=0)
    per_round = [selected * keep[0, 0][..., None].astype(jnp.float32)]
    outgoing = jnp.stack(per_round, axis=0)
    summed_first = lax.psum_scatter(outgoing, "win", scatter_dimension=3, tiled=True)
    stacked = lax.all_to_all(summed_first, "chan", split_axis=1, concat_axis=1, tiled=True)
    return stacked[None]


def solution(mesh):
    placed = (
        P(("grp", "chan"), None, "win"),
        P(("grp", "chan"), "win"),
        P("grp", None),
        P("grp", "chan", None, None),
        P("grp", "chan", None, None),
    )
    return jax.shard_map(
        shards,
        mesh=mesh,
        in_specs=placed,
        out_specs=P(("grp", "chan"), None, None, None, ("win", "rep")),
        check_vma=False,
    )
```

profile of v0, /device:TPU:0, one launch (start us, length us, event | category | flops | bytes accessed | tf_op | source)
XLA Modules:
  0.0 496.2 jit_solution(7819379614275092201)
XLA Ops:
  18.9 83.0 %all-reduce.3.cloned.1.call-done = (bf16[256,2048]{1,0:T(8,128)(2,1)}, bf16[256,2048]{1,0:T(8,128)(2,1)}) async-done(((bf16[256,2048]{1,0:T(8,128)(2,1)}, bf16[256,2048]{1,0:T(8,128)(2,1)}), (bf16[256,2048]{1,0:T(8,128)(2,1)}, bf16[256,2048]{1,0:T(8,128)(2,1)})) %all-reduce.3.cloned.1.call-update) | async-done | bytes 2097168 | tf_op jit(solution)/shard_map/psum | solution.py:13
  109.4 132.8 %while.15 = (s32[]{:T(128)}, f32[512,4,1024]{0,2,1:T(8,128)}, s32[]{:T(128)}, bf16[4,4096]{1,0:T(4,128)(2,1)S(1)}, bf16[512,2048]{1,0:T(8,128)(2,1)}, /*index=5*...) while((s32[]{:T(128)}, f32[512,4,1024]{0,2,1:T(8,128)}, ...), condition=%wide.region_3.4_spmd, body=%wide.region_2.3_spmd.sunk | while | flops 1073741824 | bytes 25407944 | solution.py:48
  116.0 5.5 %reshape.91 = bf16[4,128,2177]{2,1,0:T(8,128)(2,1)} reshape(bf16[1114624]{0:T(1024)(128)(2,1)S(1)} %reshape.90) | data formatting | bytes 4458496 | tf_op jit(solution)/shard_map/while/body/eval_jaxpr/reshape | solution.py:30
  132.5 5.5 %reshape.91 = bf16[4,128,2177]{2,1,0:T(8,128)(2,1)} reshape(bf16[1114624]{0:T(1024)(128)(2,1)S(1)} %reshape.90) | data formatting | bytes 4458496 | tf_op jit(solution)/shard_map/while/body/eval_jaxpr/reshape | solution.py:30
  138.1 4.5 fusion.20
  149.1 5.5 %reshape.91 = bf16[4,128,2177]{2,1,0:T(8,128)(2,1)} reshape(bf16[1114624]{0:T(1024)(128)(2,1)S(1)} %reshape.90) | data formatting | bytes 4458496 | tf_op jit(solution)/shard_map/while/body/eval_jaxpr/reshape | solution.py:30
  154.6 4.5 fusion.20
  165.7 5.5 %reshape.91 = bf16[4,128,2177]{2,1,0:T(8,128)(2,1)} reshape(bf16[1114624]{0:T(1024)(128)(2,1)S(1)} %reshape.90) | data formatting | bytes 4458496 | tf_op jit(solution)/shard_map/while/body/eval_jaxpr/reshape | solution.py:30
  171.2 4.5 fusion.20
  182.3 5.5 %reshape.91 = bf16[4,128,2177]{2,1,0:T(8,128)(2,1)} reshape(bf16[1114624]{0:T(1024)(128)(2,1)S(1)} %reshape.90) | data formatting | bytes 4458496 | tf_op jit(solution)/shard_map/while/body/eval_jaxpr/reshape | solution.py:30
  187.9 4.5 fusion.20
  198.9 5.5 %reshape.91 = bf16[4,128,2177]{2,1,0:T(8,128)(2,1)} reshape(bf16[1114624]{0:T(1024)(128)(2,1)S(1)} %reshape.90) | data formatting | bytes 4458496 | tf_op jit(solution)/shard_map/while/body/eval_jaxpr/reshape | solution.py:30
  204.5 4.5 fusion.20
  215.5 5.5 %reshape.91 = bf16[4,128,2177]{2,1,0:T(8,128)(2,1)} reshape(bf16[1114624]{0:T(1024)(128)(2,1)S(1)} %reshape.90) | data formatting | bytes 4458496 | tf_op jit(solution)/shard_map/while/body/eval_jaxpr/reshape | solution.py:30
  221.0 4.5 fusion.20
  232.1 5.5 %reshape.91 = bf16[4,128,2177]{2,1,0:T(8,128)(2,1)} reshape(bf16[1114624]{0:T(1024)(128)(2,1)S(1)} %reshape.90) | data formatting | bytes 4458496 | tf_op jit(solution)/shard_map/while/body/eval_jaxpr/reshape | solution.py:30
  237.6 4.5 fusion.20
  242.1 7.7 %broadcast_multiply_fusion = f32[512,4,1024]{0,2,1:T(8,128)} fusion(f32[512,4,1024]{0,2,1:T(8,128)} %get-tuple-element.140), kind=kLoop, calls=%fused_computation.9 | loop fusion | flops 2097152 | bytes 16777216 | tf_op jit(solution)/shard_map/mul | solution.py:66
  249.8 10.5 %copy.8 = f32[512,4,1024]{2,1,0:T(4,128)} copy(f32[512,4,1024]{0,2,1:T(8,128)} %broadcast_multiply_fusion) | data formatting | bytes 16777216 | tf_op jit(solution)/shard_map/mul | solution.py:66
  260.3 10.0 %mul.56 = f32[2048,1024]{1,0:T(8,128)} reshape(f32[512,4,1024]{2,1,0:T(4,128)} %copy.8) | data formatting | bytes 16777216 | tf_op jit(solution)/shard_map/mul | solution.py:66
  270.3 15.1 %gather_fusion = f32[2048,1024]{1,0:T(8,128)} fusion(f32[2048,1024]{1,0:T(8,128)} %mul.56, s32[2048]{0:T(1024)S(1)} %broadcast_clamp_fusion), kind=kCustom, calls=%fused_computation | custom fusion | bytes 16785408 | tf_op jit(solution)/shard_map/jit(_take)/gather | solution.py:67
  285.3 5.8 %select_multiply_fusion = f32[1,4,512,1024]{3,2,0,1:T(8,128)} fusion(f32[1,4,512,1024]{3,2,0,1:T(8,128)} %bitcast.45, f32[4,512]{1,0:T(4,128)S(1)} %convert_bitcast_fusion, pred[4,512]{1,0:T(4,128)(4,1)S(1)} %compare_and_fusion), kind=kLoop, calls=%fused_computation.8 | loop fusion | flops 4194304 | bytes 16787456 | tf_op jit(solution)/shard_map/mul | solution.py:68
  291.2 98.4 %reduce-scatter.2.cloned.1.call-done = f32[1,4,512,512]{3,2,0,1:T(8,128)} async-done(((f32[1,4,512,1024]{3,2,0,1:T(8,128)}), f32[1,4,512,512]{3,2,0,1:T(8,128)}) %reduce-scatter.2.cloned.1.call-update) | async-done | bytes 4194320 | tf_op jit(solution)/shard_map/reduce_scatter | solution.py:70
  389.6 97.7 %all_to_all.5 = f32[1,4,512,512]{3,2,0,1:T(8,128)S(1)} all-to-all(f32[1,4,512,512]{3,2,0,1:T(8,128)} %reduce-scatter.2.cloned.1.call-done), channel_id=1, replica_groups=mesh['grp'=2,'chan'=4,'win'=2,'rep'=2] {'chan'}, dimensions={1} | all-to-all | bytes 8388608 | tf_op jit(solution)/shard_map/all_to_all | solution.py:71
  (58 shorter events, 77.4 us)
Async XLA Ops:
  6.5 95.4 %all-reduce.3.cloned.1.call-start = ((), (), s32[]{:S(2)}) async-start(), calls=%async_computation.3 | async-start | bytes 4194304 | tf_op jit(solution)/shard_map/psum | solution.py:13
  12.0 377.6 %reduce-scatter.2.cloned.1.call-start = ((), (), s32[]{:S(2)}) async-start(), calls=%async_computation.2 | async-start | bytes 12582912 | tf_op jit(solution)/shard_map/reduce_scatter | solution.py:70
  12.1 6.1 %collective-permute-start = (bf16[4,2048]{1,0:T(4,128)(2,1)}, bf16[4,2048]{1,0:T(4,128)(2,1)S(1)}, u32[]{:S(2)}, u32[]{:S(2)}) collective-permute-start(bf16[4,2048]{1,0:T(4,128)(2,1)} %param.8), channel_id=1, source_target_pairs={{2,0},{3,1},{6,4},{7,5},{10,8},{11,9},{14,12},{15,13},{18,16},{19,... | collective-permute-start | bytes 49160 | tf_op jit(solution)/shard_map/ppermute | solution.py:19
Sparse Core Ops, SparseCore 0:
  12.1 89.7 all-reduce.2
  291.3 98.2 reduce-scatter.1
where the time goes:
time: 497 us; the launch traced here: 496 us
  waiting for transfers between devices  184 us (37%)
  local copies, waits for them, and re-layouts  140 us (28%)
  blocking collectives  97.7 us (20%)
  matrix products  35.8 us (7%)
  other arithmetic  22.2 us (4%)
  between operations  14.8 us (3%)
    reduce_scatter x1, waiting for transfers between devices, shards(): lax.psum_scatter(outgoing, 'win', scatter_dimension=3, tiled=True)  98.4 us
    all_to_all x1, blocking collectives, shards(): lax.all_to_all(summed_first, 'chan', split_axis=1, concat_axis=1, tiled=T...  97.7 us
    psum x1, waiting for transfers between devices, broadcast(): return lax.psum(kept, axis)  83 us
    reshape x8, local copies, waits for them, and re-layouts, lag_tile(): tiled[:, :lag_block * (span + 1)].reshape(rows, lag_block, span + 1)  44.3 us
    dot_general x8, matrix products, lag_step(): jnp.einsum('st,rkt->srk', source_rows, toeplitz, preferred_element_type=j...  35.8 us
    while x24, local copies, waits for them, and re-layouts  33.6 us
    mul x2, local copies, waits for them, and re-layouts, shards(): flattened = corr.reshape(-1, lag_dev) * norming  20.5 us
    slice x8, local copies, waits for them, and re-layouts, lag_tile(): tiled[:, :lag_block * (span + 1)].reshape(rows, lag_block, span + 1)  18.2 us
  transfers between devices with their start and end apart: 3, of which 3 were waited for; matrix products, arithmetic and copies ran while one was open for 1% of the time, Pallas kernels for 0%

commit v1 on v0

v1 whole, which is shorter than its diff:
```python
import functools
import math

import jax
import jax.numpy as jnp
from jax import lax
from jax.experimental import pallas as pl
from jax.experimental.pallas import tpu as pltpu
from jax.sharding import PartitionSpec as P

LAGS = 2048
LANES = 128
SHIFT_ROWS = 8
STEP = 2 * LANES
HANKEL_BYTES = 24 * 2**20
VMEM_BYTES = 48 * 2**20


def moved(block, axis, distance):
    devices = range(lax.axis_size(axis))
    route = [(i, i + distance) for i in devices if i + distance in devices]
    return lax.ppermute(block, axis, route)


def turned(block, axis, distance):
    size = lax.axis_size(axis)
    return lax.ppermute(block, axis, [(i, (i + distance) % size) for i in range(size)])


def hankel_rows(base, width):
    length = base.shape[1]
    rows = []
    for first in range(0, LANES, 2 * SHIFT_ROWS):
        both = []
        for shift in (first, first + SHIFT_ROWS):
            rolled = base if shift == 0 else pltpu.roll(base, length - shift, 1)
            both.append(rolled[:, :width])
        rows.append(jnp.concatenate(both, axis=0).astype(jnp.bfloat16))
    return jnp.concatenate(rows, axis=0)


def hankel_kernel(base_ref, out_ref):
    out_ref[0, 0] = hankel_rows(base_ref[0, 0], out_ref.shape[3])


def build_hankel(bases, width):
    channels, spans, rows, length = bases.shape
    return pl.pallas_call(
        hankel_kernel,
        grid=(channels, spans),
        in_specs=[pl.BlockSpec((1, 1, rows, length), lambda i, j: (i, j, 0, 0))],
        out_specs=pl.BlockSpec((1, 1, LANES, width), lambda i, j: (i, j, 0, 0)),
        out_shape=jax.ShapeDtypeStruct((channels, spans, LANES, width), jnp.bfloat16),
        cost_estimate=pl.CostEstimate(
            flops=channels * spans * LANES * width * 2,
            bytes_accessed=channels * spans * LANES * width * 2,
            transcendentals=0,
        ),
        compiler_params=pltpu.CompilerParams(vmem_limit_bytes=VMEM_BYTES // 2),
        name="hankel",
    )(bases)


def correlate_kernel(
    spans, halves, tile, norming, prebuilt, first, passes_ref, counts_ref, *refs
):
    pieces = refs[: spans * halves]
    signal_ref, row_ref, code_ref = refs[spans * halves : spans * halves + 3]
    rest = refs[spans * halves + 3 :]
    if not first:
        before_ref, rest = rest[0], rest[1:]
    out_ref, gathered, high, low = rest[:4]
    r_dev = signal_ref.shape[0]
    samples = pieces[0].shape[1]
    lag_dev = out_ref.shape[2]
    width = samples - LANES + lag_dev
    half_rows = pieces[0].shape[0]
    group = pl.program_id(0)

    if not prebuilt:
        hankel_ref = rest[4]
        for r in range(r_dev):
            for v in range(spans):
                hankel_ref[r, v] = hankel_rows(signal_ref[r, v], width)
    else:
        hankel_ref = signal_ref

    if first:
        out_ref[0] = jnp.zeros(out_ref.shape[1:], jnp.float32)
    else:
        out_ref[0] = before_ref[0]

    def one_pass(number, carry):
        for r in range(r_dev):
            slots = slice(r * tile, (r + 1) * tile)
            needed = counts_ref[group * r_dev + r] > number * tile

            @pl.when(needed)
            def _():
                start = pl.multiple_of((number * r_dev + r) * tile, 8)
                rows = row_ref[0, pl.ds(start, tile), :]
                lanes = lax.broadcasted_iota(jnp.int32, (tile, half_rows * halves), 1)
                pick = jnp.where(rows == lanes, 1.0, 0.0).astype(jnp.bfloat16)
                total = jnp.zeros((tile, lag_dev), jnp.float32)
                for v in range(spans):
                    for t in range(0, samples, STEP):
                        block = jnp.concatenate(
                            [pieces[v * halves + u][:, t : t + STEP] for u in range(halves)], axis=0
                        )
                        chosen = jnp.dot(pick, block, preferred_element_type=jnp.float32)
                        gathered[:, v * samples + t : v * samples + t + STEP] = chosen.astype(jnp.bfloat16)
                for v in range(spans):
                    for t in range(0, samples, STEP):
                        wide = jnp.concatenate(
                            [
                                hankel_ref[r, v, :, t : t + lag_dev],
                                hankel_ref[r, v, :, t + LANES : t + LANES + lag_dev],
                            ],
                            axis=0,
                        )
                        total += jnp.dot(
                            gathered[:, v * samples + t : v * samples + t + STEP],
                            wide,
                            preferred_element_type=jnp.float32,
                        )
                total = total * norming
                upper = total.astype(jnp.bfloat16)
                high[slots, :] = upper
                low[slots, :] = (total - upper.astype(jnp.float32)).astype(jnp.bfloat16)

            @pl.when(jnp.logical_not(needed))
            def _():
                high[slots, :] = jnp.zeros((tile, lag_dev), jnp.bfloat16)
                low[slots, :] = jnp.zeros((tile, lag_dev), jnp.bfloat16)

        codes = code_ref[0]
        lanes = lax.broadcasted_iota(jnp.int32, (codes.shape[0], r_dev * tile), 1)
        place = jnp.where(codes == lanes + number * (r_dev * tile), 1.0, 0.0).astype(jnp.bfloat16)
        out_ref[0] += jnp.dot(place, high[...], preferred_element_type=jnp.float32) + jnp.dot(
            place, low[...], preferred_element_type=jnp.float32
        )
        return carry

    lax.fori_loop(0, passes_ref[group], one_pass, 0)


def correlate(pieces, signal, prebuilt, rows, codes, passes, counts, before, tile, norming, lag_dev):
    spans, halves = len(pieces), len(pieces[0])
    flat = [piece for span in pieces for piece in span]
    groups, cap = codes.shape[:2]
    r_dev = signal.shape[0] // groups
    samples = flat[0].shape[1]
    first = before is None
    whole = lambda i, *_: (0, 0)
    in_specs = [pl.BlockSpec(piece.shape, whole) for piece in flat]
    in_specs.append(pl.BlockSpec((r_dev,) + signal.shape[1:], lambda i, *_: (i, 0, 0, 0)))
    in_specs.append(pl.BlockSpec((1,) + rows.shape[1:], lambda i, *_: (i, 0, 0)))
    in_specs.append(pl.BlockSpec((1,) + codes.shape[1:], lambda i, *_: (i, 0, 0)))
    args = flat + [signal, rows, codes]
    aliases = {}
    if not first:
        in_specs.append(pl.BlockSpec((1, cap, lag_dev), lambda i, *_: (i, 0, 0)))
        args.append(before)
        aliases = {len(args) + 1: 0}
    scratch = [
        pltpu.VMEM((tile, spans * samples), jnp.bfloat16),
        pltpu.VMEM((r_dev * tile, lag_dev), jnp.bfloat16),
        pltpu.VMEM((r_dev * tile, lag_dev), jnp.bfloat16),
    ]
    if not prebuilt:
        scratch.append(pltpu.VMEM((r_dev, spans, LANES, samples - LANES + lag_dev), jnp.bfloat16))
    body = functools.partial(correlate_kernel, spans, halves, tile, norming, prebuilt, first)
    return pl.pallas_call(
        body,
        grid_spec=pltpu.PrefetchScalarGridSpec(
            num_scalar_prefetch=2,
            grid=(groups,),
            in_specs=in_specs,
            out_specs=pl.BlockSpec((1, cap, lag_dev), lambda i, *_: (i, 0, 0)),
            scratch_shapes=scratch,
        ),
        out_shape=jax.ShapeDtypeStruct((groups, cap, lag_dev), jnp.float32),
        input_output_aliases=aliases,
        cost_estimate=pl.CostEstimate(
            flops=2 * groups * r_dev * tile * spans * samples * (lag_dev + halves * flat[0].shape[0]),
            bytes_accessed=signal.size * signal.dtype.itemsize + groups * cap * lag_dev * 4,
            transcendentals=0,
        ),
        compiler_params=pltpu.CompilerParams(vmem_limit_bytes=VMEM_BYTES),
        name="correlate",
    )(passes, counts, *args)


def shards(sources, receivers, plan, pair_index, keep):
    _, block_rows, samples = sources.shape
    r_dev = receivers.shape[0]
    n_chan = lax.axis_size("chan")
    n_win = lax.axis_size("win")
    n_rep = lax.axis_size("rep")
    chan, win, rep = lax.axis_index("chan"), lax.axis_index("win"), lax.axis_index("rep")
    cap = pair_index.shape[3]
    lag_dev = LAGS // (n_win * n_rep)
    half_rows = block_rows // n_rep
    tile = max(16, cap // 8)
    norming = 1.0 / math.sqrt(samples * n_win)

    packed = pair_index[0, 0] * 2 + keep[0, 0]
    lists = lax.all_to_all(packed, "chan", split_axis=0, concat_axis=0, tiled=True)

    heard = lax.all_gather(receivers, ("chan", "win"))
    heard = heard.reshape(n_chan, n_win, r_dev, samples).transpose(0, 2, 1, 3)
    heard = heard.reshape(n_chan * r_dev, n_win * samples)
    heard = jnp.pad(heard, ((0, 0), (0, LAGS + SHIFT_ROWS)))
    lag_start = (win * n_rep + rep) * lag_dev
    bases = []
    for v in range(n_win):
        begin = (win + n_win - v) % n_win * samples + lag_start
        span = lax.dynamic_slice_in_dim(heard, begin, samples + lag_dev + SHIFT_ROWS, 1)
        shifted = [span[:, i : i + samples + lag_dev] for i in range(SHIFT_ROWS)]
        bases.append(jnp.stack(shifted, axis=1))
    bases = jnp.stack(bases, axis=1).astype(jnp.float32)
    width = samples - LANES + lag_dev
    prebuilt = n_chan * r_dev * n_win * LANES * width * 2 <= HANKEL_BYTES
    signal = build_hankel(bases, width) if prebuilt else bases

    distance = jnp.abs(plan[0] - chan)
    nearer = jnp.where(distance[0] <= distance[1], 0, 1)
    owners = [jnp.where(nearer == 0, plan[0, 0], plan[0, 1]), jnp.where(nearer == 0, plan[0, 1], plan[0, 0])]

    pairs, kept = lists // 2, lists % 2
    source_row, receiver = pairs // r_dev, pairs % r_dev
    position = source_row // block_rows
    row = (source_row % block_rows + block_rows - rep * half_rows) % block_rows
    most = min(block_rows, cap)
    n_pass = -(-most // tile)
    turn = jnp.where(position == nearer, 0, 1)
    segments = turn * r_dev + receiver
    member = (segments[:, None, :] == jnp.arange(2 * r_dev)[None, :, None]) & (kept[:, None, :] == 1)
    below = (jnp.arange(cap)[:, None] < jnp.arange(cap)[None, :]).astype(jnp.bfloat16)
    before = jnp.einsum(
        "csi,ij->csj", member.astype(jnp.bfloat16), below, preferred_element_type=jnp.float32
    ).astype(jnp.int32)
    rank = jnp.sum(jnp.where(member, before, 0), axis=1)
    slot = rank // tile * (r_dev * tile) + receiver * tile + rank % tile
    counts = jnp.sum(member.astype(jnp.int32), axis=2)

    own = lax.dynamic_slice_in_dim(sources[0], rep * half_rows, half_rows, 0)
    arrived = {0: own}
    lower = upper = own
    for step in range(1, n_chan):
        lower = moved(lower, "chan", 1)
        upper = moved(upper, "chan", -1)
        arrived[-step], arrived[step] = lower, upper

    result = None
    for q in range(2):
        where = owners[q] - chan
        chosen = own
        reach = n_chan - 1 if q else n_chan - 2
        for offset in range(-reach, reach + 1):
            if offset:
                chosen = jnp.where(where == offset, arrived[offset], chosen)
        spans = [chosen] + [turned(chosen, "win", v) for v in range(1, n_win)]
        pieces = [[piece] + [turned(piece, "rep", -u) for u in range(1, n_rep)] for piece in spans]
        mine = (turn == q) & (kept == 1)
        codes = jnp.where(mine, slot, -1)
        slots = jnp.arange(n_pass * r_dev * tile)
        rows = jnp.sum(jnp.where(codes[:, None, :] == slots[None, :, None], row[:, None, :], 0), axis=2)
        of_turn = counts[:, q * r_dev : (q + 1) * r_dev]
        passes = -(-jnp.max(of_turn, axis=1) // tile)
        result = correlate(
            pieces, signal, prebuilt, rows[..., None], codes[..., None], passes, of_turn.reshape(-1), result,
            tile, norming, lag_dev,
        )
    return result[None, None]


def solution(mesh):
    placed = (
        P(("grp", "chan"), None, "win"),
        P(("grp", "chan"), "win"),
        P("grp", None),
        P("grp", "chan", None, None),
        P("grp", "chan", None, None),
    )
    return jax.shard_map(
        shards,
        mesh=mesh,
        in_specs=placed,
        out_specs=P(("grp", "chan"), None, None, None, ("win", "rep")),
        check_vma=False,
    )
```

time: 497 us -> 183 us (0.37)
  waiting for transfers between devices: 184 us -> 20.2 us
  local copies, waits for them, and re-layouts: 140 us -> 21.9 us
  blocking collectives: 97.7 us -> 32 us
  Pallas kernels: 0 us -> 60.9 us
  matrix products: 35.8 us -> 0.21 us
  starting transfers between devices: 1.34 us -> 27.9 us
  between operations: 14.8 us -> 4.05 us
  other arithmetic: 22.2 us -> 14 us
    reduce_scatter x1 -> x0, waiting for transfers between devices: 98.4 us -> none  [shards(): lax.psum_scatter(outgoing, 'win', scatter_dimension=3, tiled=True)]
    all_to_all x1 -> x0, blocking collectives: 97.7 us -> none  [shards(): lax.all_to_all(summed_first, 'chan', split_axis=1, concat_axis=1, tiled=T...]
    psum x1 -> x0, waiting for transfers between devices: 83 us -> none  [broadcast(): return lax.psum(kept, axis)]
    pallas_call x0 -> x3, Pallas kernels: none -> 60.9 us  [the longest x2 53.2 us: correlate(): pl.pallas_call(body, grid_spec=pltpu.PrefetchScalarGridSpec(num_scalar_pr...]
    reshape x8 -> x3, local copies, waits for them, and re-layouts: 44.3 us -> 0.3 us  [the longest x2 0.16 us: shards(): of_turn.reshape(-1)]
    dot_general x8 -> x1, matrix products: 35.8 us -> 0.21 us  [shards(): jnp.einsum('csi,ij->csj', member.astype(jnp.bfloat16), below, preferred_e...]
    while x24 -> x0, local copies, waits for them, and re-layouts: 33.6 us -> none
    all_gather x0 -> x1, blocking collectives: none -> 32 us  [shards(): heard = lax.all_gather(receivers, ('chan', 'win'))]
  transfers between devices with their start and end apart: 3 -> 13, of which waited for: 3 -> 6; matrix products, arithmetic and copies ran while one was open for 1% -> 14% of each run, Pallas kernels for 0% -> 19%
where the time goes in v1:
time: 183 us; the launch traced here: 181 us
  Pallas kernels  60.9 us (33%)
  blocking collectives  32 us (17%)
  starting transfers between devices  27.9 us (15%)
  local copies, waits for them, and re-layouts  21.9 us (12%)
  waiting for transfers between devices  20.2 us (11%)
  other arithmetic  14 us (8%)
  between operations  4.05 us (2%)
    pallas_call x2, Pallas kernels, correlate(): pl.pallas_call(body, grid_spec=pltpu.PrefetchScalarGridSpec(num_scalar_pr...  53.2 us
    all_gather x1, blocking collectives, shards(): heard = lax.all_gather(receivers, ('chan', 'win'))  32 us
    ppermute x6, starting transfers between devices, moved(): return lax.ppermute(block, axis, route)  20.8 us
    ppermute x6, waiting for transfers between devices, turned(): lax.ppermute(block, axis, [(i, (i + distance) % size) for i in range(size)])  11.6 us
    another operation x20, local copies, waits for them, and re-layouts, shards(): bases.append(jnp.stack(shifted, axis=1))  8.76 us
    ppermute x6, waiting for transfers between devices, moved(): return lax.ppermute(block, axis, route)  8.59 us
    pallas_call x1, Pallas kernels, build_hankel(): pl.pallas_call(hankel_kernel, grid=(channels, spans), in_specs=[pl.BlockS...  7.71 us
    unnamed x11, local copies, waits for them, and re-layouts  6.8 us
  transfers between devices with their start and end apart: 13, of which 6 were waited for; matrix products, arithmetic and copies ran while one was open for 14% of the time, Pallas kernels for 19%

profile of v1, /device:TPU:0, one launch (start us, length us, event | category | flops | bytes accessed | tf_op | source)
XLA Modules:
  0.0 181.3 jit_solution(4387765409786577744)
XLA Ops:
  0.0 1.9 %dynamic-slice_bitcast_fusion = bf16[128,2048]{1,0:T(8,128)(2,1)} fusion(bf16[1,256,2048]{2,1,0:T(8,128)(2,1)} %param.5, s32[]{:T(128)S(6)} %select_n.336), kind=kLoop, calls=%fused_computation.64 | loop fusion | bytes 1048580 | tf_op jit(solution)/shard_map/dynamic_slice | solution.py:247
  3.2 6.4 %collective-permute-start.3 = (bf16[128,2048]{1,0:T(8,128)(2,1)}, bf16[128,2048]{1,0:T(8,128)(2,1)}, u32[]{:S(2)}, u32[]{:S(2)}) collective-permute-start(bf16[128,2048]{1,0:T(8,128)(2,1)} %dynamic-slice_bitcast_fusion), channel_id=1, source_target_pairs={{0,4},{4,8},{8,12},{1,5},{5,9},{9,13},{2,6},{6,10},{10,14},{3,7},{... | collective-permute-start | bytes 1572872 | tf_op jit(solution)/shard_map/ppermute | solution.py:22
  9.6 1.3 fusion.56
  10.9 4.3 %all-to-all-start = ((s32[4,1,512]{2,1,0:T(1,128)}), s32[4,1,512]{2,1,0:T(1,128)S(1)}, u32[]{:S(2)}, u32[]{:S(2)}) async-start(s32[4,1,512]{2,1,0:T(1,128)} %fusion.56), calls=%async_computation | async-start | bytes 16384 | tf_op jit(solution)/shard_map/all_to_all | solution.py:208
  15.2 32.0 %all-gather.1 = bf16[8,4,2048]{2,1,0:T(4,128)(2,1)S(1)} all-gather(bf16[1,4,2048]{2,1,0:T(4,128)(2,1)} %bitcast.81), channel_id=2, replica_groups=mesh['grp'=2,'chan'=4,'win'=2,'rep'=2] {'chan','win'}, dimensions={0}, use_global_device_ids=true | all-gather | bytes 147456 | tf_op jit(solution)/shard_map/all_gather | solution.py:210
  51.5 2.1 %stack.71 = bf16[16,8,2560]{2,1,0:T(8,128)(2,1)S(1)} concatenate(bf16[16,1,2560]{2,1,0:T(2,128)(2,1)S(1)} %copy.445, bf16[16,1,2560]{2,1,0:T(2,128)(2,1)S(1)} %copy.446, bf16[16,1,2560]{2,1,0:T(2,128)(2,1)S(1)} %copy.447, bf16[16,1,2560]{2,1,0:T(2,128)(2,1)S(1)} %copy.448, bf16[16,1,2560]{2,1,0:T(2,128)(2,1)S(1)} %copy.449, bf16[16,1,2560]{2,1,0:T(2,128)(2,1)S(1)} %copy.450, ...), dimensions={1} | concatenate | bytes 1310720 | tf_op jit(solution)/shard_map/stack | solution.py:220
  53.7 3.2 %stack.81 = bf16[16,8,2560]{2,1,0:T(8,128)(2,1)} concatenate(bf16[16,1,2560]{2,1,0:T(2,128)(2,1)S(1)} %copy.453, bf16[16,1,2560]{2,1,0:T(2,128)(2,1)S(1)} %copy.454, bf16[16,1,2560]{2,1,0:T(2,128)(2,1)S(1)} %copy.455, bf16[16,1,2560]{2,1,0:T(2,128)(2,1)S(1)} %copy.456, bf16[16,1,2560]{2,1,0:T(2,128)(2,1)S(1)} %copy.457, bf16[16,1,2560]{2,1,0:T(2,128)(2,1)S(1)} %copy.458, ...), dimensions={1} | concatenate | bytes 1310720 | tf_op jit(solution)/shard_map/stack | solution.py:220
  62.4 7.7 %hankel.1.refs_4_ = bf16[16,2,128,2432]{3,2,1,0:T(8,128)(2,1)S(1)} custom-call(f32[16,2,8,2560]{3,2,1,0:T(8,128)S(1)} %maximum_convert_fusion.base_ref), custom_call_target="tpu_custom_call" | custom-call | flops 19922944 | bytes 19922944 | tf_op jit(solution)/shard_map/hankel/pallas_call | solution.py:48
  70.1 6.7 %copy-done = bf16[16,2,128,2432]{3,2,1,0:T(8,128)(2,1)} copy-done((bf16[16,2,128,2432]{3,2,1,0:T(8,128)(2,1)}, bf16[16,2,128,2432]{3,2,1,0:T(8,128)(2,1)S(1)}, u32[]{:S(2)}) %copy-start) | copy-done | bytes 19922968
  77.5 1.3 collective-permute-start.1
  78.9 5.4 %collective-permute-start.4 = (bf16[128,2048]{1,0:T(8,128)(2,1)}, bf16[128,2048]{1,0:T(8,128)(2,1)}, u32[]{:S(2)}, u32[]{:S(2)}) collective-permute-start(bf16[128,2048]{1,0:T(8,128)(2,1)} %collective-permute-done.3), channel_id=1, source_target_pairs={{0,4},{4,8},{8,12},{1,5},{5,9},{9,13},{2,6},{6,10},{10,14},{3,7},{... | collective-permute-start | bytes 1572872 | tf_op jit(solution)/shard_map/ppermute | solution.py:22
  84.2 2.2 %select_reduce_fusion = (s32[4,1024]{1,0:T(4,128)S(1)}, s32[4,1024]{1,0:T(4,128)S(1)}) fusion(s32[4,512]{1,0:T(4,128)S(1)} %bitcast.78, s32[4,512]{1,0:T(4,128)S(1)} %get-tuple-element.49, s32[4,512]{1,0:T(4,128)S(1)} %get-tuple-element.50), kind=kLoop, calls=%fused_computation | loop fusion | flops 12574720 | bytes 57344 | tf_op jit(solution)/shard_map/reduce_sum | solution.py:268
  87.4 4.8 %collective-permute-done.1 = bf16[128,2048]{1,0:T(8,128)(2,1)} collective-permute-done((bf16[128,2048]{1,0:T(8,128)(2,1)}, bf16[128,2048]{1,0:T(8,128)(2,1)}, u32[]{:S(2)}, u32[]{:S(2)}) %collective-permute-start.1) | collective-permute-done | bytes 524320 | tf_op jit(solution)/shard_map/ppermute | solution.py:22
  93.7 5.2 %collective-permute-start.5 = (bf16[128,2048]{1,0:T(8,128)(2,1)}, bf16[128,2048]{1,0:T(8,128)(2,1)}, u32[]{:S(2)}, u32[]{:S(2)}) collective-permute-start(bf16[128,2048]{1,0:T(8,128)(2,1)} %collective-permute-done.4), channel_id=1, source_target_pairs={{0,4},{4,8},{8,12},{1,5},{5,9},{9,13},{2,6},{6,10},{10,14},{3,7},{... | collective-permute-start | bytes 1572872 | tf_op jit(solution)/shard_map/ppermute | solution.py:22
  99.3 2.0 %copy.470.refs_5_ = s32[4,1024,1]{2,1,0:T(8,128)} copy(s32[4,1024,1]{1,0,2:T(4,128)S(1)} %bitcast.75) | data formatting | bytes 32768 | tf_op jit(solution)/shard_map/broadcast_in_dim | solution.py:272
  101.4 2.1 %collective-permute-done.2 = bf16[128,2048]{1,0:T(8,128)(2,1)} collective-permute-done((bf16[128,2048]{1,0:T(8,128)(2,1)}, bf16[128,2048]{1,0:T(8,128)(2,1)}, u32[]{:S(2)}, u32[]{:S(2)}) %collective-permute-start.2) | collective-permute-done | bytes 524320 | tf_op jit(solution)/shard_map/ppermute | solution.py:22
  103.6 1.5 collective-permute-done.5
  105.1 2.5 %select_select_fusion = (bf16[128,2048]{1,0:T(8,128)(2,1)S(1)}, bf16[128,2048]{1,0:T(8,128)(2,1)S(1)}) fusion(bf16[128,2048]{1,0:T(8,128)(2,1)} %collective-permute-done.1, bf16[128,2048]{1,0:T(8,128)(2,1)} %collective-permute-done, bf16[128,2048]{1,0:T(8,128)(2,1)} %collective-permute-done.3, bf16[128,2048]{1,0:T(8,128)(2,1)} %collective-permute-done.4, ...), kind=kLoop, calls=%fused_computation.62 | loop fusion | flops 2621440 | bytes 4718606 | tf_op jit(solution)/shard_map/jit(_where)/select_n | solution.py:262
  108.6 3.6 %fusion.29 = (s32[4,512,1]{2,1,0:T(8,128)S(1)}, s32[4,512,1]{2,1,0:T(8,128)S(1)}) fusion(s32[4,512]{1,0:T(4,128)S(1)} %get-tuple-element.39, s32[]{:T(128)} %bitcast.1, s32[4,512,1]{2,1,0:T(8,128)S(1)} %copy.465), kind=kLoop, calls=%fused_computation.60 | loop fusion | flops 167936 | bytes 32772 | tf_op jit(solution)/shard_map/jit(_where)/select_n | solution.py:266
  113.4 4.8 %collective-permute-done.10.refs_2_ = bf16[128,2048]{1,0:T(8,128)(2,1)S(1)} collective-permute-done((bf16[128,2048]{1,0:T(8,128)(2,1)S(1)}, bf16[128,2048]{1,0:T(8,128)(2,1)S(1)}, u32[]{:S(2)}, u32[]{:S(2)}) %collective-permute-start.10) | collective-permute-done | bytes 524320 | tf_op jit(solution)/shard_map/ppermute | solution.py:27
  118.2 2.4 %fusion.27.refs_6_ = s32[4,512,1]{2,1,0:T(8,128)S(1)} fusion(s32[4,512,1]{2,1,0:T(8,128)S(1)} %get-tuple-element.10, s32[4,512]{1,0:T(4,128)S(1)} %get-tuple-element.39, s32[]{:T(128)} %bitcast.1), kind=kLoop, calls=%fused_computation.58 | loop fusion | flops 112640 | bytes 24580 | tf_op jit(solution)/shard_map/jit(_where)/select_n | solution.py:266
  121.2 6.8 %collective-permute-done.7.refs_2_ = bf16[128,2048]{1,0:T(8,128)(2,1)S(1)} collective-permute-done((bf16[128,2048]{1,0:T(8,128)(2,1)S(1)}, bf16[128,2048]{1,0:T(8,128)(2,1)S(1)}, u32[]{:S(2)}, u32[]{:S(2)}) %collective-permute-start.7) | collective-permute-done | bytes 524320 | tf_op jit(solution)/shard_map/ppermute | solution.py:27
  128.1 26.4 %correlate.2.refs_7_ = f32[4,512,512]{2,1,0:T(8,128)} custom-call(s32[4]{0:T(128)S(1)} %get-tuple-element.47.passes_ref, s32[16]{0:T(128)S(1)} %reshape.462.counts_ref, bf16[128,2048]{1,0:T(8,128)(2,1)S(1)} %get-tuple-element.21.refs_0_, bf16[128,2048]{1,0:T(8,128)(2,1)S(1)} %collective-permute-done.9.refs_1_, ...), custom_call_target="tpu_custom_call" | custom-call | flops 6442450944 | bytes 24117248 | tf_op jit(solution)/shard_map/correlate/pallas_call | solution.py:173
  154.6 26.8 %correlate.3 = f32[4,512,512]{2,1,0:T(8,128)} custom-call(s32[4]{0:T(128)S(1)} %get-tuple-element.48.passes_ref, s32[16]{0:T(128)S(1)} %reshape.459.counts_ref, bf16[128,2048]{1,0:T(8,128)(2,1)S(1)} %get-tuple-element.22.refs_0_, bf16[128,2048]{1,0:T(8,128)(2,1)S(1)} %collective-permute-done.6.refs_1_, ...), custom_call_target="tpu_custom_call", output_to_operand_aliasing={{}: (9, {})} | custom-call | flops 6442450944 | bytes 24117248 | tf_op jit(solution)/shard_map/correlate/pallas_call | solution.py:173
  (63 shorter events, 13.7 us)
Async XLA Ops:
  0.0 51.0 %copy-start.2 = (s32[1,2]{1,0:T(1,128)S(1)}, s32[1,2]{1,0:T(1,128)}, u32[]{:S(2)}) copy-start(s32[1,2]{1,0:T(1,128)} %param.7) | copy-start | bytes 28
  1.9 75.6 %collective-permute-start = (bf16[128,2048]{1,0:T(8,128)(2,1)}, bf16[128,2048]{1,0:T(8,128)(2,1)}, u32[]{:S(2)}, u32[]{:S(2)}) collective-permute-start(bf16[128,2048]{1,0:T(8,128)(2,1)} %dynamic-slice_bitcast_fusion), channel_id=1, source_target_pairs={{4,0},{8,4},{12,8},{5,1},{9,5},{13,9},{6,2},{10,6},{14,10},{7,3},{... | collective-permute-start | bytes 1572872 | tf_op jit(solution)/shard_map/ppermute | solution.py:22
  3.2 75.6 %collective-permute-start.3 = (bf16[128,2048]{1,0:T(8,128)(2,1)}, bf16[128,2048]{1,0:T(8,128)(2,1)}, u32[]{:S(2)}, u32[]{:S(2)}) collective-permute-start(bf16[128,2048]{1,0:T(8,128)(2,1)} %dynamic-slice_bitcast_fusion), channel_id=1, source_target_pairs={{0,4},{4,8},{8,12},{1,5},{5,9},{9,13},{2,6},{6,10},{10,14},{3,7},{... | collective-permute-start | bytes 1572872 | tf_op jit(solution)/shard_map/ppermute | solution.py:22
  10.9 66.0 %all-to-all-start = ((s32[4,1,512]{2,1,0:T(1,128)}), s32[4,1,512]{2,1,0:T(1,128)S(1)}, u32[]{:S(2)}, u32[]{:S(2)}) async-start(s32[4,1,512]{2,1,0:T(1,128)} %fusion.56), calls=%async_computation | async-start | bytes 16384 | tf_op jit(solution)/shard_map/all_to_all | solution.py:208
  70.1 6.7 %copy-start = (bf16[16,2,128,2432]{3,2,1,0:T(8,128)(2,1)}, bf16[16,2,128,2432]{3,2,1,0:T(8,128)(2,1)S(1)}, u32[]{:S(2)}) copy-start(bf16[16,2,128,2432]{3,2,1,0:T(8,128)(2,1)S(1)} %hankel.1.refs_4_) | copy-start | bytes 59768836
  77.5 14.7 %collective-permute-start.1 = (bf16[128,2048]{1,0:T(8,128)(2,1)}, bf16[128,2048]{1,0:T(8,128)(2,1)}, u32[]{:S(2)}, u32[]{:S(2)}) collective-permute-start(bf16[128,2048]{1,0:T(8,128)(2,1)} %collective-permute-done), channel_id=1, source_target_pairs={{4,0},{8,4},{12,8},{5,1},{9,5},{13,9},{6,2},{10,6},{14,10},{7,3},{... | collective-permute-start | bytes 1572872 | tf_op jit(solution)/shard_map/ppermute | solution.py:22
  78.9 14.8 %collective-permute-start.4 = (bf16[128,2048]{1,0:T(8,128)(2,1)}, bf16[128,2048]{1,0:T(8,128)(2,1)}, u32[]{:S(2)}, u32[]{:S(2)}) collective-permute-start(bf16[128,2048]{1,0:T(8,128)(2,1)} %collective-permute-done.3), channel_id=1, source_target_pairs={{0,4},{4,8},{8,12},{1,5},{5,9},{9,13},{2,6},{6,10},{10,14},{3,7},{... | collective-permute-start | bytes 1572872 | tf_op jit(solution)/shard_map/ppermute | solution.py:22
  92.2 11.4 %collective-permute-start.2 = (bf16[128,2048]{1,0:T(8,128)(2,1)}, bf16[128,2048]{1,0:T(8,128)(2,1)}, u32[]{:S(2)}, u32[]{:S(2)}) collective-permute-start(bf16[128,2048]{1,0:T(8,128)(2,1)} %collective-permute-done.1), channel_id=1, source_target_pairs={{4,0},{8,4},{12,8},{5,1},{9,5},{13,9},{6,2},{10,6},{14,10},{7,3},{... | collective-permute-start | bytes 1572872 | tf_op jit(solution)/shard_map/ppermute | solution.py:22
  93.7 11.4 %collective-permute-start.5 = (bf16[128,2048]{1,0:T(8,128)(2,1)}, bf16[128,2048]{1,0:T(8,128)(2,1)}, u32[]{:S(2)}, u32[]{:S(2)}) collective-permute-start(bf16[128,2048]{1,0:T(8,128)(2,1)} %collective-permute-done.4), channel_id=1, source_target_pairs={{0,4},{4,8},{8,12},{1,5},{5,9},{9,13},{2,6},{6,10},{10,14},{3,7},{... | collective-permute-start | bytes 1572872 | tf_op jit(solution)/shard_map/ppermute | solution.py:22
  107.6 10.6 %collective-permute-start.10 = (bf16[128,2048]{1,0:T(8,128)(2,1)S(1)}, bf16[128,2048]{1,0:T(8,128)(2,1)S(1)}, u32[]{:S(2)}, u32[]{:S(2)}) collective-permute-start(bf16[128,2048]{1,0:T(8,128)(2,1)S(1)} %get-tuple-element.21.refs_0_), channel_id=1, source_target_pairs={{0,2},{2,0},{1,3},{3,1},{4,6},{6,4},{5,7},{7,5},{8,10},{10,8},{9,1... | collective-permute-start | bytes 1572872 | tf_op jit(solution)/shard_map/ppermute | solution.py:27
  112.2 15.9 %collective-permute-start.9 = (bf16[128,2048]{1,0:T(8,128)(2,1)S(1)}, bf16[128,2048]{1,0:T(8,128)(2,1)S(1)}, u32[]{:S(2)}, u32[]{:S(2)}) collective-permute-start(bf16[128,2048]{1,0:T(8,128)(2,1)S(1)} %get-tuple-element.21.refs_0_), channel_id=1, source_target_pairs={{0,1},{1,0},{2,3},{3,2},{4,5},{5,4},{6,7},{7,6},{8,9},{9,8},{10,11... | collective-permute-start | bytes 1572872 | tf_op jit(solution)/shard_map/ppermute | solution.py:27
  112.3 15.8 %collective-permute-start.7 = (bf16[128,2048]{1,0:T(8,128)(2,1)S(1)}, bf16[128,2048]{1,0:T(8,128)(2,1)S(1)}, u32[]{:S(2)}, u32[]{:S(2)}) collective-permute-start(bf16[128,2048]{1,0:T(8,128)(2,1)S(1)} %get-tuple-element.22.refs_0_), channel_id=1, source_target_pairs={{0,2},{2,0},{1,3},{3,1},{4,6},{6,4},{5,7},{7,5},{8,10},{10,8},{9,1... | collective-permute-start | bytes 1572872 | tf_op jit(solution)/shard_map/ppermute | solution.py:27
  118.2 9.9 %collective-permute-start.11 = (bf16[128,2048]{1,0:T(8,128)(2,1)S(1)}, bf16[128,2048]{1,0:T(8,128)(2,1)S(1)}, u32[]{:S(2)}, u32[]{:S(2)}) collective-permute-start(bf16[128,2048]{1,0:T(8,128)(2,1)S(1)} %collective-permute-done.10.refs_2_), channel_id=1, source_target_pairs={{0,1},{1,0},{2,3},{3,2},{4,5},{5,4},{6,7},{7,6},{8,9},{9,8},{10,11... | collective-permute-start | bytes 1572872 | tf_op jit(solution)/shard_map/ppermute | solution.py:27
  120.7 33.9 %collective-permute-start.6 = (bf16[128,2048]{1,0:T(8,128)(2,1)S(1)}, bf16[128,2048]{1,0:T(8,128)(2,1)S(1)}, u32[]{:S(2)}, u32[]{:S(2)}) collective-permute-start(bf16[128,2048]{1,0:T(8,128)(2,1)S(1)} %get-tuple-element.22.refs_0_), channel_id=1, source_target_pairs={{0,1},{1,0},{2,3},{3,2},{4,5},{5,4},{6,7},{7,6},{8,9},{9,8},{10,11... | collective-permute-start | bytes 1572872 | tf_op jit(solution)/shard_map/ppermute | solution.py:27
  128.1 26.5 %collective-permute-start.8 = (bf16[128,2048]{1,0:T(8,128)(2,1)S(1)}, bf16[128,2048]{1,0:T(8,128)(2,1)S(1)}, u32[]{:S(2)}, u32[]{:S(2)}) collective-permute-start(bf16[128,2048]{1,0:T(8,128)(2,1)S(1)} %collective-permute-done.7.refs_2_), channel_id=1, source_target_pairs={{0,1},{1,0},{2,3},{3,2},{4,5},{5,4},{6,7},{7,6},{8,9},{9,8},{10,11... | collective-permute-start | bytes 1572872 | tf_op jit(solution)/shard_map/ppermute | solution.py:27
  128.1 26.5 %copy-start.1 = (s32[4,1024,1]{2,1,0:T(8,128)S(1)}, s32[4,1024,1]{2,1,0:T(8,128)}, u32[]{:S(2)}) copy-start(s32[4,1024,1]{2,1,0:T(8,128)} %copy.470.refs_5_) | copy-start | bytes 49156
